TPU v7x, 32 devices: a whole 2x2x4 slice. The times are simulated.
32 devices in a mesh: vir: 8 (over y, x, core), out: 4 (over z).
Axes of the slice: x: 2, y: 2, z: 4, core: 2. Of those that a mesh axis runs over, the one named last changes fastest.
Arguments:
- factors: bfloat16 [512, 512, 1536], P('out', 'vir'), may hold values from -2.5 to 2.5
- amplitudes: bfloat16 [128, 512, 512], P('out', 'vir'), may hold values from -0.015991211 to 0.015991211
Outputs:
- ladder: float32 [2, 128, 512], P(None, 'vir', 'out')
All inputs are finite; a program needn't handle non-finite values.
Results may differ from a plain program's by a relative error of at most 0.0029.
Values may be sent and summed in bfloat16 or wider, within the bound.
No kernel may reach another device: no remote copies, remote signals or barrier semaphores. Data moves between devices by JAX's collectives and lax.ppermute only.
A program may use at most 128 MiB of HBM per device.

v0:
```python
import functools

import jax
import jax.numpy as jnp
from jax import lax
from jax.experimental import pallas as pl
from jax.experimental.pallas import tpu as pltpu
from jax.sharding import PartitionSpec as P

BB = 2
LANES = 128
NT = (((1,), (1,)), ((), ()))
NN = (((1,), (0,)), ((), ()))
LITTLE = pl.CostEstimate(flops=1024, bytes_accessed=1024, transcendentals=0)


def largest_part(extent, limit):
    part = min(extent, limit)
    while extent % part:
        part -= 1
    return part


def call(kernel, inputs, in_specs, out_shape, out_spec, through, grid=(1,), scratch=(), vmem=28):
    n_in, n_thru = len(inputs), len(through)

    def run(*refs):
        outs = refs[n_in + n_thru :]
        kernel(*refs[:n_in], outs[0], *outs[1 + n_thru :])

    anywhere = pl.BlockSpec(memory_space=pl.ANY)
    out = pl.pallas_call(
        run,
        grid=grid,
        in_specs=list(in_specs) + [anywhere] * n_thru,
        out_specs=[out_spec] + [anywhere] * n_thru,
        out_shape=[out_shape] + [jax.ShapeDtypeStruct(t.shape, t.dtype) for t in through],
        input_output_aliases={n_in + k: 1 + k for k in range(n_thru)},
        scratch_shapes=list(scratch),
        compiler_params=pltpu.CompilerParams(vmem_limit_bytes=vmem * 2**20),
        cost_estimate=LITTLE,
    )(*inputs, *through)
    return out[0], list(out[1:])


def fixed(array):
    anywhere = pl.BlockSpec(memory_space=pl.ANY)
    return pl.pallas_call(
        lambda *refs: None,
        in_specs=[anywhere],
        out_specs=anywhere,
        out_shape=jax.ShapeDtypeStruct(array.shape, array.dtype),
        input_output_aliases={0: 0},
        cost_estimate=LITTLE,
    )(array)


def pack_kernel(*refs):
    for k, slab in enumerate(refs[:-1]):
        refs[-1][k] = slab[...]


def pack(slabs, through):
    vmem = pl.BlockSpec(memory_space=pltpu.VMEM)
    shape = jax.ShapeDtypeStruct((len(slabs),) + slabs[0].shape, slabs[0].dtype)
    return call(pack_kernel, slabs, [vmem] * len(slabs), shape, vmem, through)


def assemble_kernel(*refs):
    place_ref, packs, out_ref, whole_ref = refs[0], refs[1:-2], refs[-2], refs[-1]
    piece = packs[0].shape[2]
    for i, packed in enumerate(packs):
        for k in range(packed.shape[0]):
            start = pl.multiple_of(place_ref[i * packed.shape[0] + k] * piece, piece)
            whole_ref[:, pl.ds(start, piece), :] = packed[k]
    for b in range(out_ref.shape[0]):
        out_ref[b] = whole_ref[b].T


def assemble(packs, places, through):
    count, bb, piece, aux_len = packs[0].shape
    d_len = piece * count * len(packs)
    vmem = pl.BlockSpec(memory_space=pltpu.VMEM)
    return call(
        assemble_kernel,
        [places] + packs,
        [pl.BlockSpec(memory_space=pltpu.SMEM)] + [vmem] * len(packs),
        jax.ShapeDtypeStruct((bb, aux_len, d_len), jnp.bfloat16),
        vmem,
        through,
        scratch=[pltpu.VMEM((bb, d_len, aux_len), jnp.bfloat16)],
    )


def integral_kernel(factor_ref, batch_ref, out_ref):
    a_len, c_len, aux_len = factor_ref.shape
    d_len = out_ref.shape[3]
    rows = factor_ref[...].reshape(a_len * c_len, aux_len)
    wide = largest_part(d_len // LANES, 2) * LANES
    for b in range(out_ref.shape[1]):
        for j in range(0, d_len, wide):
            tile = lax.dot_general(
                rows, batch_ref[b, :, j : j + wide], NN, preferred_element_type=jnp.float32
            )
            turned = jnp.swapaxes(tile.reshape(a_len, c_len, wide), 0, 1)
            out_ref[:, b, :, j : j + wide] = turned.astype(jnp.bfloat16)


def integrals(factors, batch, start, stop, through):
    a_rows, c_rows, aux_len = factors.shape
    bb, _, d_len = batch.shape
    c_len = largest_part(c_rows, 8)
    first = start // c_len
    return call(
        integral_kernel,
        [factors, batch],
        [
            pl.BlockSpec((a_rows, c_len, aux_len), lambda i: (0, first + i, 0)),
            pl.BlockSpec((bb, aux_len, d_len), lambda i: (0, 0, 0)),
        ],
        jax.ShapeDtypeStruct((stop - start, bb, a_rows, d_len), jnp.bfloat16),
        pl.BlockSpec((c_len, bb, a_rows, d_len), lambda i: (i, 0, 0, 0)),
        through,
        grid=((stop - start) // c_len,),
    )


def ladder_kernel(count, *refs):
    tau_refs, (integral_ref, out_ref, total_ref) = refs[:count], refs[count:]
    c_len, bb, a_rows, d_len = integral_ref.shape
    step = pl.program_id(0)

    @pl.when(step == 0)
    def _():
        total_ref[...] = jnp.zeros_like(total_ref)

    total = total_ref[...]
    for c in range(c_len):
        left = integral_ref[c].reshape(bb * a_rows, d_len)
        right = jnp.concatenate([r[i, c] for r in tau_refs for i in range(r.shape[0])], axis=0)
        total += lax.dot_general(left, right, NT, preferred_element_type=jnp.float32)
    total_ref[...] = total

    @pl.when(step == pl.num_programs(0) - 1)
    def _():
        out_ref[...] = total_ref[...].T


def ladder_terms(taus, integral, through):
    _, c_rows, pairs, d_len = taus[0].shape
    _, bb, a_rows, _ = integral.shape
    c_len = largest_part(c_rows, 8)
    places = [t.shape[0] for t in taus]
    shape = (bb * a_rows, sum(places) * pairs)
    return call(
        functools.partial(ladder_kernel, len(taus)),
        taus + [integral],
        [pl.BlockSpec((k, c_len, pairs, d_len), lambda i: (0, i, 0, 0)) for k in places]
        + [pl.BlockSpec((c_len, bb, a_rows, d_len), lambda i: (i, 0, 0, 0))],
        jax.ShapeDtypeStruct(shape[::-1], jnp.float32),
        pl.BlockSpec(shape[::-1], lambda i: (0, 0)),
        through,
        grid=(c_rows // c_len,),
        scratch=[pltpu.VMEM(shape, jnp.float32)],
        vmem=16,
    )


def spread(rows, n, z):
    stride = 1
    while 2 * stride < n:
        stride *= 2
    while stride:
        ways = [(i, i + stride) for i in range(0, n - stride, 2 * stride)]
        here = lax.ppermute(rows, "out", ways)
        taking = functools.reduce(jnp.logical_or, [z == t for _, t in ways])
        rows = jnp.where(taking, here, rows)
        stride //= 2
    return rows


def everywhere(shared, vir, through):
    me = lax.axis_index("vir")

    def swap(array, mask):
        return lax.ppermute(array, "vir", [(k, k ^ mask) for k in range(vir)])

    if vir & (vir - 1) == 0 and 2 < vir <= 8:
        masks = list(range(0, vir, 2))
        slabs = [shared] + [swap(shared, m) for m in masks[1:]]
        packed, through = pack(slabs, through)
        packs = [packed, swap(packed, 1)]
        places = jnp.stack([me ^ m ^ core for core in (0, 1) for m in masks])
    else:
        packs = [lax.all_gather(shared, "vir", axis=1, tiled=True)[None]]
        places = jnp.zeros((1,), jnp.int32)
    return assemble(packs, places.astype(jnp.int32), through)


def body(inward, factors, amplitudes):
    a_rows, c_rows, _ = factors.shape
    pairs = amplitudes.shape[0]
    n = lax.axis_size("out")
    vir = lax.axis_size("vir")
    z = lax.axis_index("out")
    cut = c_rows - inward

    outer = fixed(amplitudes[:, :cut].transpose(1, 0, 2))
    tau = lax.all_gather(outer, "out")
    shared = spread(factors[:BB], n, z)
    token = jnp.zeros((8, LANES), jnp.float32)

    if inward:
        inner = amplitudes[:, cut:].transpose(1, 0, 2)
        batch, [token, inner] = everywhere(shared, vir, [token, inner])
        sent, [token] = integrals(factors, batch, cut, c_rows, [token])
        came = lax.ppermute(sent, "out", [(0, 1), (n - 1, n - 2)])
        kept, [token] = integrals(factors, batch, 0, cut, [token])
        below, above = [], []
        for k in range(1, n - 1):
            below.append(lax.ppermute(inner, "out", [(i, i + k) for i in range(n - 1 - k)]))
            above.append(lax.ppermute(inner, "out", [(i + k, i) for i in range(1, n - k)]))
        nearby = [t[None] for t in below[::-1] + [inner] + above]
        mine, [token] = ladder_terms(nearby, sent, [token])
        theirs, [token] = ladder_terms(nearby, came, [token])

        def all_pairs(terms):
            return lax.dynamic_slice_in_dim(terms, (n - 2 - z) * pairs, n * pairs, axis=0)

        back = lax.ppermute(all_pairs(theirs), "out", [(1, 0), (n - 2, n - 1)])
        rest = jnp.where((z == 0) | (z == n - 1), back, all_pairs(mine))
    else:
        batch, [token] = everywhere(shared, vir, [token])
        kept, [token] = integrals(factors, batch, 0, cut, [token])
        rest = jnp.zeros((n * pairs, BB * a_rows), jnp.float32)

    terms, _ = ladder_terms([tau], kept, [token])
    parts = (terms + rest).reshape(vir, -1, BB * a_rows)
    swapped = lax.all_to_all(parts, "vir", split_axis=0, concat_axis=0)
    out = jnp.sum(swapped, axis=0)
    return out.reshape(-1, BB, a_rows).transpose(1, 0, 2)


def solution(mesh):
    def run(factors, amplitudes):
        c_rows = factors.shape[1] // mesh.shape["vir"]
        inward = c_rows // 8 if c_rows % 64 == 0 and mesh.shape["out"] == 4 else 0
        placed = (P("out", "vir", None), P("out", "vir", None))
        return jax.shard_map(
            functools.partial(body, inward),
            mesh=mesh,
            in_specs=placed,
            out_specs=P(None, "vir", "out"),
            check_vma=False,
        )(factors, amplitudes)

    return run
```

profile of v0, /device:TPU:16, one launch (start us, length us, event | category | flops | bytes accessed | tf_op | source)
XLA Modules:
  0.0 234.9 jit_solution(2980331790844034372)
XLA Ops:
  6.5 0.0 slice-start
  6.5 0.0 all-gather.3.cloned.1.call-start
  6.5 1.5 slice-done
  8.0 1.8 copy.25
  9.9 0.0 all-gather.3.cloned.1.call-update
  9.9 0.0 slice-start.1
  9.9 1.1 slice.10
  11.0 1.3 collective-permute-start
  12.3 16.5 %collective-permute-done = bf16[2,64,1536]{2,1,0:T(8,128)(2,1)S(1)} collective-permute-done((bf16[2,64,1536]{2,1,0:T(8,128)(2,1)S(1)}, bf16[2,64,1536]{2,1,0:T(8,128)(2,1)S(1)}, u32[]{:S(2)}, u32[]{:S(2)}) %collective-permute-start) | collective-permute-done | bytes 393248 | tf_op jit(solution)/shard_map/ppermute | solution.py:175
  28.8 1.1 broadcast_select_fusion
  29.8 1.3 collective-permute-start.1
  31.2 42.2 %collective-permute-done.1 = bf16[2,64,1536]{2,1,0:T(8,128)(2,1)S(1)} collective-permute-done((bf16[2,64,1536]{2,1,0:T(8,128)(2,1)S(1)}, bf16[2,64,1536]{2,1,0:T(8,128)(2,1)S(1)}, u32[]{:S(2)}, u32[]{:S(2)}) %collective-permute-start.1) | collective-permute-done | bytes 393248 | tf_op jit(solution)/shard_map/ppermute | solution.py:175
  73.4 1.5 collective-permute-start.2
  74.9 1.5 collective-permute-start.3
  76.4 0.5 collective-permute-start.4
  76.9 0.0 slice-done.1
  76.9 0.1 copy.26
  77.0 8.5 %collective-permute-done.2.refs_1_ = bf16[2,64,1536]{2,1,0:T(8,128)(2,1)S(1)} collective-permute-done((bf16[2,64,1536]{2,1,0:T(8,128)(2,1)S(1)}, bf16[2,64,1536]{2,1,0:T(8,128)(2,1)S(1)}, u32[]{:S(2)}, u32[]{:S(2)}) %collective-permute-start.2) | collective-permute-done | bytes 393248 | tf_op jit(solution)/shard_map/ppermute | solution.py:186
  85.5 6.5 %collective-permute-done.3.refs_2_ = bf16[2,64,1536]{2,1,0:T(8,128)(2,1)S(1)} collective-permute-done((bf16[2,64,1536]{2,1,0:T(8,128)(2,1)S(1)}, bf16[2,64,1536]{2,1,0:T(8,128)(2,1)S(1)}, u32[]{:S(2)}, u32[]{:S(2)}) %collective-permute-start.3) | collective-permute-done | bytes 393248 | tf_op jit(solution)/shard_map/ppermute | solution.py:186
  92.0 0.7 collective-permute-done.4.refs_3_
  92.7 0.1 shard_map.29
  92.8 0.1 collective-permute-start.5
  92.9 0.0 copy-start.3
  92.9 1.2 copy-done.3
  94.1 0.1 stack.35.refs_0_
  94.2 2.1 collective-permute-done.5.refs_2_
  96.3 0.0 copy-start.5
  96.3 1.2 copy-done.5
  97.5 0.0 copy-start.4
  97.5 1.4 copy-done.4
  98.9 0.0 copy-start.6
  98.9 1.4 copy-done.6
  100.4 1.6 shard_map.30
  102.0 6.8 %shard_map.31 = (bf16[8,2,128,512]{3,2,1,0:T(8,128)(2,1)}, f32[8,128]{1,0:T(8,128)S(1)}) custom-call(bf16[128,64,1536]{2,1,0:T(8,128)(2,1)} %refs_0_.3, bf16[2,1536,512]{2,1,0:T(8,128)(2,1)S(1)} %get-tuple-element.23.refs_1_, f32[8,128]{1,0:T(8,128)S(1)} %get-tuple-element.24.refs_2_), custom_call_target="tpu_custom_call", output_to_operand_aliasing={{1}: (2, {})} | custom-call | flops 1024 | bytes 1024 | tf_op jit(solution)/shard_map/pallas_call | solution.py:32
  108.8 1.3 collective-permute-start.10
  110.1 1.3 collective-permute-start.6
  111.4 1.3 collective-permute-start.7
  112.7 4.6 %collective-permute-start.8 = (bf16[8,32,512]{2,1,0:T(8,128)(2,1)S(1)}, bf16[8,32,512]{2,1,0:T(8,128)(2,1)}, u32[]{:S(2)}, u32[]{:S(2)}) collective-permute-start(bf16[8,32,512]{2,1,0:T(8,128)(2,1)S(1)} %get-tuple-element.27), channel_id=1, source_target_pairs={{2,1},{3,2},{6,5},{7,6},{10,9},{11,10},{14,13},{15,14},{18,17},{19... | collective-permute-start | bytes 786440 | tf_op jit(solution)/shard_map/ppermute | solution.py:222
  117.3 1.4 collective-permute-start.9
  118.6 27.6 %shard_map.32 = (bf16[56,2,128,512]{3,2,1,0:T(8,128)(2,1)S(1)}, f32[8,128]{1,0:T(8,128)S(1)}) custom-call(bf16[128,64,1536]{2,1,0:T(8,128)(2,1)} %refs_0_.3, bf16[2,1536,512]{2,1,0:T(8,128)(2,1)S(1)} %get-tuple-element.23.refs_1_, f32[8,128]{1,0:T(8,128)S(1)} %get-tuple-element.25.refs_2_), custom_call_target="tpu_custom_call", output_to_operand_aliasing={{1}: (2, {})} | custom-call | flops 1024 | bytes 1024 | tf_op jit(solution)/shard_map/pallas_call | solution.py:32
  146.2 0.0 copy-start
  146.2 5.2 %copy-done = bf16[56,2,128,512]{3,2,1,0:T(8,128)(2,1)} copy-done((bf16[56,2,128,512]{3,2,1,0:T(8,128)(2,1)}, bf16[56,2,128,512]{3,2,1,0:T(8,128)(2,1)S(1)}, u32[]{:S(2)}) %copy-start) | copy-done | bytes 14680088
  151.4 35.9 %collective-permute-done.6 = bf16[8,32,512]{2,1,0:T(8,128)(2,1)} collective-permute-done((bf16[8,32,512]{2,1,0:T(8,128)(2,1)S(1)}, bf16[8,32,512]{2,1,0:T(8,128)(2,1)}, u32[]{:S(2)}, u32[]{:S(2)}) %collective-permute-start.6) | collective-permute-done | bytes 262176 | tf_op jit(solution)/shard_map/ppermute | solution.py:221
  187.3 0.0 collective-permute-done.7
  187.3 4.9 %collective-permute-done.8 = bf16[8,32,512]{2,1,0:T(8,128)(2,1)} collective-permute-done((bf16[8,32,512]{2,1,0:T(8,128)(2,1)S(1)}, bf16[8,32,512]{2,1,0:T(8,128)(2,1)}, u32[]{:S(2)}, u32[]{:S(2)}) %collective-permute-start.8) | collective-permute-done | bytes 262176 | tf_op jit(solution)/shard_map/ppermute | solution.py:222
  192.2 0.0 collective-permute-done.9
  192.2 2.7 %shard_map.33 = (f32[160,256]{1,0:T(8,128)S(1)}, f32[8,128]{1,0:T(8,128)S(1)}) custom-call(bf16[1,8,32,512]{3,2,1,0:T(8,128)(2,1)} %bitcast.11.refs_0_, bf16[1,8,32,512]{3,2,1,0:T(8,128)(2,1)} %bitcast.12.refs_1_, bf16[1,8,32,512]{3,2,1,0:T(8,128)(2,1)S(1)} %bitcast.24, bf16[1,8,32,512]{3,2,1,0:T(8,128)(2,1)} %bitcast.14.refs_3_, ...), custom_call_target="tpu_custom_call", output_to_operand_aliasing={{1}: (6, {})} | custom-call | flops 1024 | bytes 1024 | tf_op jit(solution)/shard_map/pallas_call | solution.py:32
  194.9 0.0 collective-permute-done.10.refs_5_
  194.9 2.7 %shard_map.34 = (f32[160,256]{1,0:T(8,128)S(1)}, f32[8,128]{1,0:T(8,128)S(1)}) custom-call(bf16[1,8,32,512]{3,2,1,0:T(8,128)(2,1)} %bitcast.11.refs_0_, bf16[1,8,32,512]{3,2,1,0:T(8,128)(2,1)} %bitcast.12.refs_1_, bf16[1,8,32,512]{3,2,1,0:T(8,128)(2,1)S(1)} %bitcast.25, bf16[1,8,32,512]{3,2,1,0:T(8,128)(2,1)} %bitcast.14.refs_3_, ...), custom_call_target="tpu_custom_call", output_to_operand_aliasing={{1}: (6, {})} | custom-call | flops 1024 | bytes 1024 | tf_op jit(solution)/shard_map/pallas_call | solution.py:32
  197.7 6.8 %collective-permute-start.11 = (f32[128,256]{1,0:T(8,128)S(1)}, f32[128,256]{1,0:T(8,128)S(1)}, u32[]{:S(2)}, u32[]{:S(2)}) collective-permute-start(f32[128,256]{1,0:T(8,128)S(1)} %constant_dynamic-slice_fusion), channel_id=1, source_target_pairs={{1,0},{2,3},{5,4},{6,7},{9,8},{10,11},{13,12},{14,15},{17,16},{18,... | collective-permute-start | bytes 393224 | tf_op jit(solution)/shard_map/ppermute | solution.py:230
  204.5 0.0 all-gather.3.cloned.1.call-done
  204.5 0.0 copy-start.1
  204.6 5.2 %copy-done.1 = bf16[56,2,128,512]{3,2,1,0:T(8,128)(2,1)S(1)} copy-done((bf16[56,2,128,512]{3,2,1,0:T(8,128)(2,1)S(1)}, bf16[56,2,128,512]{3,2,1,0:T(8,128)(2,1)}, u32[]{:S(2)}) %copy-start.1) | copy-done | bytes 14680088
  209.7 0.0 copy-start.2
  209.7 3.1 %copy-done.2 = bf16[224,32,512]{2,1,0:T(8,128)(2,1)S(1)} copy-done((bf16[224,32,512]{2,1,0:T(8,128)(2,1)S(1)}, bf16[224,32,512]{2,1,0:T(8,128)(2,1)}, u32[]{:S(2)}) %copy-start.2) | copy-done | bytes 7340056
  212.8 5.6 %shard_map.35 = (f32[128,256]{1,0:T(8,128)S(1)}, f32[8,128]{1,0:T(8,128)S(1)}) custom-call(bf16[4,56,32,512]{3,2,1,0:T(8,128)(2,1)S(1)} %bitcast.22, bf16[56,2,128,512]{3,2,1,0:T(8,128)(2,1)S(1)} %copy-done.1, f32[8,128]{1,0:T(8,128)S(1)} %get-tuple-element.31.refs_2_), custom_call_target="tpu_custom_call", output_to_operand_aliasing={{1}: (2, {})} | custom-call | flops 1024 | bytes 1024 | tf_op jit(solution)/shard_map/pallas_call | solution.py:32
  218.4 0.0 collective-permute-done.11
  218.5 8.9 %all_to_all.5 = f32[8,16,256]{2,1,0:T(8,128)S(1)} all-to-all(f32[8,16,256]{2,1,0:T(8,128)S(1)} %bitcast.27), channel_id=1, replica_groups=mesh['vir'=8,'out'=4] {'vir'}, dimensions={0} | all-to-all | bytes 262144 | tf_op jit(solution)/shard_map/all_to_all | solution.py:239
  227.5 0.6 copy.20
  (7 shorter events, 0.1 us)
Async XLA Ops:
  6.5 1.5 slice-start
  6.5 198.0 %all-gather.3.cloned.1.call-start = ((), (), s32[]{:S(2)}) async-start(), calls=%async_computation.1 | async-start | bytes 9175040 | tf_op jit(solution)/shard_map/all_gather | solution.py:209
  9.9 67.0 %slice-start.1 = ((bf16[32,64,512]{2,1,0:T(8,128)(2,1)}), bf16[32,8,512]{2,1,0:T(8,128)(2,1)S(1)}, s32[]{:S(2)}) async-start(bf16[32,64,512]{2,1,0:T(8,128)(2,1)} %param.3), calls=%async_computation.3 | async-start | bytes 524288 | tf_op jit(solution)/shard_map/slice | solution.py:214
  11.0 17.8 %collective-permute-start = (bf16[2,64,1536]{2,1,0:T(8,128)(2,1)S(1)}, bf16[2,64,1536]{2,1,0:T(8,128)(2,1)S(1)}, u32[]{:S(2)}, u32[]{:S(2)}) collective-permute-start(bf16[2,64,1536]{2,1,0:T(8,128)(2,1)S(1)} %slice.10), channel_id=1, source_target_pairs={{0,2},{4,6},{8,10},{12,14},{16,18},{20,22},{24,26},{28,30}} | collective-permute-start | bytes 1179656 | tf_op jit(solution)/shard_map/ppermute | solution.py:175
  29.8 43.5 %collective-permute-start.1 = (bf16[2,64,1536]{2,1,0:T(8,128)(2,1)S(1)}, bf16[2,64,1536]{2,1,0:T(8,128)(2,1)S(1)}, u32[]{:S(2)}, u32[]{:S(2)}) collective-permute-start(bf16[2,64,1536]{2,1,0:T(8,128)(2,1)S(1)} %broadcast_select_fusion), channel_id=1, source_target_pairs={{0,1},{2,3},{4,5},{6,7},{8,9},{10,11},{12,13},{14,15},{16,17},{18,... | collective-permute-start | bytes 1179656 | tf_op jit(solution)/shard_map/ppermute | solution.py:175
  73.4 12.1 %collective-permute-start.2 = (bf16[2,64,1536]{2,1,0:T(8,128)(2,1)S(1)}, bf16[2,64,1536]{2,1,0:T(8,128)(2,1)S(1)}, u32[]{:S(2)}, u32[]{:S(2)}) collective-permute-start(bf16[2,64,1536]{2,1,0:T(8,128)(2,1)S(1)} %broadcast_select_fusion.1.refs_0_), channel_id=1, source_target_pairs={{0,8},{4,12},{8,0},{12,4},{16,24},{20,28},{24,16},{28,20},{1,9},{5... | collective-permute-start | bytes 1179656 | tf_op jit(solution)/shard_map/ppermute | solution.py:186
  74.9 17.1 %collective-permute-start.3 = (bf16[2,64,1536]{2,1,0:T(8,128)(2,1)S(1)}, bf16[2,64,1536]{2,1,0:T(8,128)(2,1)S(1)}, u32[]{:S(2)}, u32[]{:S(2)}) collective-permute-start(bf16[2,64,1536]{2,1,0:T(8,128)(2,1)S(1)} %broadcast_select_fusion.1.refs_0_), channel_id=1, source_target_pairs={{0,16},{4,20},{8,24},{12,28},{16,0},{20,4},{24,8},{28,12},{1,17},{... | collective-permute-start | bytes 1179656 | tf_op jit(solution)/shard_map/ppermute | solution.py:186
  76.4 16.3 %collective-permute-start.4 = (bf16[2,64,1536]{2,1,0:T(8,128)(2,1)S(1)}, bf16[2,64,1536]{2,1,0:T(8,128)(2,1)S(1)}, u32[]{:S(2)}, u32[]{:S(2)}) collective-permute-start(bf16[2,64,1536]{2,1,0:T(8,128)(2,1)S(1)} %broadcast_select_fusion.1.refs_0_), channel_id=1, source_target_pairs={{0,24},{4,28},{8,16},{12,20},{16,8},{20,12},{24,0},{28,4},{1,25},{... | collective-permute-start | bytes 1179656 | tf_op jit(solution)/shard_map/ppermute | solution.py:186
  92.8 3.5 %collective-permute-start.5 = (bf16[4,2,64,1536]{3,2,1,0:T(8,128)(2,1)S(1)}, bf16[4,2,64,1536]{3,2,1,0:T(8,128)(2,1)S(1)}, u32[]{:S(2)}, u32[]{:S(2)}) collective-permute-start(bf16[4,2,64,1536]{3,2,1,0:T(8,128)(2,1)S(1)} %get-tuple-element.20.refs_1_), channel_id=1, source_target_pairs={{0,4},{4,0},{8,12},{12,8},{16,20},{20,16},{24,28},{28,24},{1,5},{5... | collective-permute-start | bytes 4718600 | tf_op jit(solution)/shard_map/ppermute | solution.py:186
  92.9 1.2 copy-start.3
  96.3 1.2 copy-start.5
  97.5 1.4 copy-start.4
  98.9 1.4 copy-start.6
  108.8 86.1 %collective-permute-start.10 = (bf16[8,2,128,512]{3,2,1,0:T(8,128)(2,1)}, bf16[8,2,128,512]{3,2,1,0:T(8,128)(2,1)}, u32[]{:S(2)}, u32[]{:S(2)}) collective-permute-start(bf16[8,2,128,512]{3,2,1,0:T(8,128)(2,1)} %get-tuple-element.28.refs_5_), channel_id=1, source_target_pairs={{0,1},{3,2},{4,5},{7,6},{8,9},{11,10},{12,13},{15,14},{16,17},{19,... | collective-permute-start | bytes 6291464 | tf_op jit(solution)/shard_map/ppermute | solution.py:217
  110.1 77.2 %collective-permute-start.6 = (bf16[8,32,512]{2,1,0:T(8,128)(2,1)S(1)}, bf16[8,32,512]{2,1,0:T(8,128)(2,1)}, u32[]{:S(2)}, u32[]{:S(2)}) collective-permute-start(bf16[8,32,512]{2,1,0:T(8,128)(2,1)S(1)} %get-tuple-element.27), channel_id=1, source_target_pairs={{0,2},{4,6},{8,10},{12,14},{16,18},{20,22},{24,26},{28,30}} | collective-permute-start | bytes 786440 | tf_op jit(solution)/shard_map/ppermute | solution.py:221
  111.4 75.9 %collective-permute-start.7 = (bf16[8,32,512]{2,1,0:T(8,128)(2,1)S(1)}, bf16[8,32,512]{2,1,0:T(8,128)(2,1)}, u32[]{:S(2)}, u32[]{:S(2)}) collective-permute-start(bf16[8,32,512]{2,1,0:T(8,128)(2,1)S(1)} %get-tuple-element.27), channel_id=1, source_target_pairs={{0,1},{1,2},{4,5},{5,6},{8,9},{9,10},{12,13},{13,14},{16,17},{17,1... | collective-permute-start | bytes 786440 | tf_op jit(solution)/shard_map/ppermute | solution.py:221
  112.7 79.5 %collective-permute-start.8 = (bf16[8,32,512]{2,1,0:T(8,128)(2,1)S(1)}, bf16[8,32,512]{2,1,0:T(8,128)(2,1)}, u32[]{:S(2)}, u32[]{:S(2)}) collective-permute-start(bf16[8,32,512]{2,1,0:T(8,128)(2,1)S(1)} %get-tuple-element.27), channel_id=1, source_target_pairs={{2,1},{3,2},{6,5},{7,6},{10,9},{11,10},{14,13},{15,14},{18,17},{19... | collective-permute-start | bytes 786440 | tf_op jit(solution)/shard_map/ppermute | solution.py:222
  117.3 74.9 %collective-permute-start.9 = (bf16[8,32,512]{2,1,0:T(8,128)(2,1)S(1)}, bf16[8,32,512]{2,1,0:T(8,128)(2,1)}, u32[]{:S(2)}, u32[]{:S(2)}) collective-permute-start(bf16[8,32,512]{2,1,0:T(8,128)(2,1)S(1)} %get-tuple-element.27), channel_id=1, source_target_pairs={{3,1},{7,5},{11,9},{15,13},{19,17},{23,21},{27,25},{31,29}} | collective-permute-start | bytes 786440 | tf_op jit(solution)/shard_map/ppermute | solution.py:222
  146.2 5.2 %copy-start = (bf16[56,2,128,512]{3,2,1,0:T(8,128)(2,1)}, bf16[56,2,128,512]{3,2,1,0:T(8,128)(2,1)S(1)}, u32[]{:S(2)}) copy-start(bf16[56,2,128,512]{3,2,1,0:T(8,128)(2,1)S(1)} %get-tuple-element.26.refs_1_) | copy-start | bytes 44040196
  197.7 20.7 %collective-permute-start.11 = (f32[128,256]{1,0:T(8,128)S(1)}, f32[128,256]{1,0:T(8,128)S(1)}, u32[]{:S(2)}, u32[]{:S(2)}) collective-permute-start(f32[128,256]{1,0:T(8,128)S(1)} %constant_dynamic-slice_fusion), channel_id=1, source_target_pairs={{1,0},{2,3},{5,4},{6,7},{9,8},{10,11},{13,12},{14,15},{17,16},{18,... | collective-permute-start | bytes 393224 | tf_op jit(solution)/shard_map/ppermute | solution.py:230
  204.5 5.2 %copy-start.1 = (bf16[56,2,128,512]{3,2,1,0:T(8,128)(2,1)S(1)}, bf16[56,2,128,512]{3,2,1,0:T(8,128)(2,1)}, u32[]{:S(2)}) copy-start(bf16[56,2,128,512]{3,2,1,0:T(8,128)(2,1)} %copy-done) | copy-start | bytes 44040196
  209.7 3.1 %copy-start.2 = (bf16[224,32,512]{2,1,0:T(8,128)(2,1)S(1)}, bf16[224,32,512]{2,1,0:T(8,128)(2,1)}, u32[]{:S(2)}) copy-start(bf16[224,32,512]{2,1,0:T(8,128)(2,1)} %all-gather.3.cloned.1.call-done) | copy-start | bytes 22020100
Sparse Core Ops, SparseCore 0:
  10.0 192.8 all-gather.2
where the time goes:
time: 239 us; the launch traced here: 235 us
  waiting for transfers between devices  117 us (49%)
  Pallas kernels  47.3 us (20%)
  local copies, waits for them, and re-layouts  23.9 us (10%)
  starting transfers between devices  22.8 us (10%)
  between operations  13.6 us (6%)
  blocking collectives  8.94 us (4%)
    ppermute x2, waiting for transfers between devices, spread(): here = lax.ppermute(rows, 'out', ways)  58.6 us
    pallas_call x7, Pallas kernels, call(): pl.pallas_call(run, grid=grid, in_specs=list(in_specs) + [anywhere] * n_t...  47.3 us
    ppermute x2, waiting for transfers between devices, body(): lax.ppermute(inner, 'out', [(i, i + k) for i in range(n - 1 - k)])  35.9 us
    unnamed x16, local copies, waits for them, and re-layouts  20.6 us
    ppermute x4, waiting for transfers between devices, swap(): return lax.ppermute(array, 'vir', [(k, k ^ mask) for k in range(vir)])  17.8 us
    all_to_all x1, blocking collectives, body(): swapped = lax.all_to_all(parts, 'vir', split_axis=0, concat_axis=0)  8.94 us
    ppermute x1, starting transfers between devices, body(): back = lax.ppermute(all_pairs(theirs), 'out', [(1, 0), (n - 2, n - 1)])  6.78 us
    ppermute x2, starting transfers between devices, body(): lax.ppermute(inner, 'out', [(i + k, i) for i in range(1, n - k)])  5.93 us
  transfers between devices with their start and end apart: 13, of which 8 were waited for; matrix products, arithmetic and copies ran while one was open for 1% of the time, Pallas kernels for 20%

commit v1 on v0

--- a/solution.py
+++ b/solution.py
@@ -43,18 +43,6 @@
     return out[0], list(out[1:])
 
 
-def fixed(array):
-    anywhere = pl.BlockSpec(memory_space=pl.ANY)
-    return pl.pallas_call(
-        lambda *refs: None,
-        in_specs=[anywhere],
-        out_specs=anywhere,
-        out_shape=jax.ShapeDtypeStruct(array.shape, array.dtype),
-        input_output_aliases={0: 0},
-        cost_estimate=LITTLE,
-    )(array)
-
-
 def pack_kernel(*refs):
     for k, slab in enumerate(refs[:-1]):
         refs[-1][k] = slab[...]
@@ -125,43 +113,94 @@
     )
 
 
-def ladder_kernel(count, *refs):
-    tau_refs, (integral_ref, out_ref, total_ref) = refs[:count], refs[count:]
+def sums(tau_of, integral_ref, total_ref):
     c_len, bb, a_rows, d_len = integral_ref.shape
-    step = pl.program_id(0)
-
-    @pl.when(step == 0)
+
+    @pl.when(pl.program_id(0) == 0)
     def _():
         total_ref[...] = jnp.zeros_like(total_ref)
 
     total = total_ref[...]
     for c in range(c_len):
         left = integral_ref[c].reshape(bb * a_rows, d_len)
-        right = jnp.concatenate([r[i, c] for r in tau_refs for i in range(r.shape[0])], axis=0)
-        total += lax.dot_general(left, right, NT, preferred_element_type=jnp.float32)
+        total += lax.dot_general(left, tau_of(c), NT, preferred_element_type=jnp.float32)
     total_ref[...] = total
 
-    @pl.when(step == pl.num_programs(0) - 1)
+
+def early_kernel(count, *refs):
+    tau_refs, (integral_ref, out_ref, total_ref) = refs[:count], refs[count:]
+    sums(
+        lambda c: jnp.concatenate([r[c] for r in tau_refs], axis=0),
+        integral_ref,
+        total_ref,
+    )
+
+    @pl.when(pl.program_id(0) == pl.num_programs(0) - 1)
     def _():
         out_ref[...] = total_ref[...].T
 
 
-def ladder_terms(taus, integral, through):
-    _, c_rows, pairs, d_len = taus[0].shape
+def late_kernel(count, *refs):
+    slot_ref, early_ref, refs = refs[0], refs[1], refs[2:]
+    tau_refs, (integral_ref, out_ref, total_ref, all_ref) = refs[:count], refs[count:]
+    pairs = tau_refs[0].shape[1]
+    sums(
+        lambda c: jnp.concatenate([r[c] for r in tau_refs], axis=0),
+        integral_ref,
+        total_ref,
+    )
+
+    @pl.when(pl.program_id(0) == pl.num_programs(0) - 1)
+    def _():
+        known = early_ref.shape[0]
+        all_ref[:known] = early_ref[...]
+        all_ref[known:] = total_ref[...].T
+        for j in range(out_ref.shape[0] // pairs):
+            start = pl.multiple_of(slot_ref[j] * pairs, pairs)
+            out_ref[j * pairs : (j + 1) * pairs] = all_ref[pl.ds(start, pairs), :]
+
+
+def ladder_specs(taus, integral):
+    c_rows, pairs, d_len = taus[0].shape
     _, bb, a_rows, _ = integral.shape
     c_len = largest_part(c_rows, 8)
-    places = [t.shape[0] for t in taus]
-    shape = (bb * a_rows, sum(places) * pairs)
-    return call(
-        functools.partial(ladder_kernel, len(taus)),
+    specs = [pl.BlockSpec((c_len, pairs, d_len), lambda i: (i, 0, 0)) for _ in taus]
+    specs.append(pl.BlockSpec((c_len, bb, a_rows, d_len), lambda i: (i, 0, 0, 0)))
+    return specs, (bb * a_rows, len(taus) * pairs), (c_rows // c_len,)
+
+
+def ladder_early(taus, integral, through):
+    specs, shape, grid = ladder_specs(taus, integral)
+    return call(
+        functools.partial(early_kernel, len(taus)),
         taus + [integral],
-        [pl.BlockSpec((k, c_len, pairs, d_len), lambda i: (0, i, 0, 0)) for k in places]
-        + [pl.BlockSpec((c_len, bb, a_rows, d_len), lambda i: (i, 0, 0, 0))],
+        specs,
         jax.ShapeDtypeStruct(shape[::-1], jnp.float32),
         pl.BlockSpec(shape[::-1], lambda i: (0, 0)),
         through,
-        grid=(c_rows // c_len,),
+        grid=grid,
         scratch=[pltpu.VMEM(shape, jnp.float32)],
+        vmem=16,
+    )
+
+
+def ladder_late(slots, early, taus, integral, through):
+    specs, shape, grid = ladder_specs(taus, integral)
+    pairs = taus[0].shape[1]
+    out = (slots.shape[0] * pairs, shape[0])
+    return call(
+        functools.partial(late_kernel, len(taus)),
+        [slots, early] + taus + [integral],
+        [pl.BlockSpec(memory_space=pltpu.SMEM), pl.BlockSpec(early.shape, lambda i: (0, 0))]
+        + specs,
+        jax.ShapeDtypeStruct(out, jnp.float32),
+        pl.BlockSpec(out, lambda i: (0, 0)),
+        through,
+        grid=grid,
+        scratch=[
+            pltpu.VMEM(shape, jnp.float32),
+            pltpu.VMEM((early.shape[0] + shape[1], shape[0]), jnp.float32),
+        ],
         vmem=16,
     )
 
@@ -197,61 +236,44 @@
     return assemble(packs, places.astype(jnp.int32), through)
 
 
-def body(inward, factors, amplitudes):
+def body(factors, amplitudes):
     a_rows, c_rows, _ = factors.shape
-    pairs = amplitudes.shape[0]
     n = lax.axis_size("out")
     vir = lax.axis_size("vir")
     z = lax.axis_index("out")
-    cut = c_rows - inward
-
-    outer = fixed(amplitudes[:, :cut].transpose(1, 0, 2))
-    tau = lax.all_gather(outer, "out")
-    shared = spread(factors[:BB], n, z)
-    token = jnp.zeros((8, LANES), jnp.float32)
-
-    if inward:
-        inner = amplitudes[:, cut:].transpose(1, 0, 2)
-        batch, [token, inner] = everywhere(shared, vir, [token, inner])
-        sent, [token] = integrals(factors, batch, cut, c_rows, [token])
-        came = lax.ppermute(sent, "out", [(0, 1), (n - 1, n - 2)])
-        kept, [token] = integrals(factors, batch, 0, cut, [token])
-        below, above = [], []
-        for k in range(1, n - 1):
-            below.append(lax.ppermute(inner, "out", [(i, i + k) for i in range(n - 1 - k)]))
-            above.append(lax.ppermute(inner, "out", [(i + k, i) for i in range(1, n - k)]))
-        nearby = [t[None] for t in below[::-1] + [inner] + above]
-        mine, [token] = ladder_terms(nearby, sent, [token])
-        theirs, [token] = ladder_terms(nearby, came, [token])
-
-        def all_pairs(terms):
-            return lax.dynamic_slice_in_dim(terms, (n - 2 - z) * pairs, n * pairs, axis=0)
-
-        back = lax.ppermute(all_pairs(theirs), "out", [(1, 0), (n - 2, n - 1)])
-        rest = jnp.where((z == 0) | (z == n - 1), back, all_pairs(mine))
+
+    def send(array, *ways):
+        return lax.ppermute(array, "out", ways)
+
+    own = amplitudes.transpose(1, 0, 2)
+    if n == 4:
+        first = send(amplitudes, (3, 1), (1, 0), (0, 2), (2, 3)).transpose(1, 0, 2)
+        shared = spread(factors[:BB], n, z)
+        second = send(own, (2, 0), (1, 3))
+        third = send(first, (1, 0), (2, 3))
+        middle = send(own, (2, 1), (1, 2))
+        inward = send(own, (3, 2), (0, 1))
+        early, late = [own, first, second], [third, middle, inward]
+        slots = jnp.array([[0, 1, 2, 3], [5, 0, 4, 1], [1, 4, 0, 5], [3, 2, 1, 0]], jnp.int32)[z]
     else:
-        batch, [token] = everywhere(shared, vir, [token])
-        kept, [token] = integrals(factors, batch, 0, cut, [token])
-        rest = jnp.zeros((n * pairs, BB * a_rows), jnp.float32)
-
-    terms, _ = ladder_terms([tau], kept, [token])
-    parts = (terms + rest).reshape(vir, -1, BB * a_rows)
+        shared = spread(factors[:BB], n, z)
+        gathered = lax.all_gather(own, "out")
+        early, late = [own], [gathered[k] for k in range(n)]
+        slots = jnp.arange(1, n + 1, dtype=jnp.int32)
+
+    batch, [token] = everywhere(shared, vir, [jnp.zeros((8, LANES), jnp.float32)])
+    integral, [token] = integrals(factors, batch, 0, c_rows, [token])
+    known, [token] = ladder_early(early, integral, [token])
+    total, _ = ladder_late(slots, known, late, integral, [token])
+
+    parts = total.reshape(vir, -1, BB * a_rows)
     swapped = lax.all_to_all(parts, "vir", split_axis=0, concat_axis=0)
     out = jnp.sum(swapped, axis=0)
     return out.reshape(-1, BB, a_rows).transpose(1, 0, 2)
 
 
 def solution(mesh):
-    def run(factors, amplitudes):
-        c_rows = factors.shape[1] // mesh.shape["vir"]
-        inward = c_rows // 8 if c_rows % 64 == 0 and mesh.shape["out"] == 4 else 0
-        placed = (P("out", "vir", None), P("out", "vir", None))
-        return jax.shard_map(
-            functools.partial(body, inward),
-            mesh=mesh,
-            in_specs=placed,
-            out_specs=P(None, "vir", "out"),
-            check_vma=False,
-        )(factors, amplitudes)
-
-    return run
+    placed = (P("out", "vir", None), P("out", "vir", None))
+    return jax.shard_map(
+        body, mesh=mesh, in_specs=placed, out_specs=P(None, "vir", "out"), check_vma=False
+    )

time: 239 us -> 183 us (0.77)
  the two profiles are of different devices: /device:TPU:16 before, /device:TPU:0 now
where the time goes in v1:
time: 183 us; the launch traced here: 182 us
  waiting for transfers between devices  93.4 us (51%)
  Pallas kernels  51.5 us (28%)
  starting transfers between devices  23.2 us (13%)
  blocking collectives  7.92 us (4%)
  local copies, waits for them, and re-layouts  5.17 us (3%)
    ppermute x2, waiting for transfers between devices, spread(): here = lax.ppermute(rows, 'out', ways)  56.5 us
    pallas_call x5, Pallas kernels, call(): pl.pallas_call(run, grid=grid, in_specs=list(in_specs) + [anywhere] * n_t...  51.5 us
    ppermute x5, waiting for transfers between devices, send(): return lax.ppermute(array, 'out', ways)  25 us
    ppermute x4, waiting for transfers between devices, swap(): return lax.ppermute(array, 'vir', [(k, k ^ mask) for k in range(vir)])  12 us
    ppermute x5, starting transfers between devices, send(): return lax.ppermute(array, 'out', ways)  11.7 us
    all_to_all x1, blocking collectives, body(): swapped = lax.all_to_all(parts, 'vir', split_axis=0, concat_axis=0)  7.92 us
    ppermute x2, starting transfers between devices, spread(): here = lax.ppermute(rows, 'out', ways)  7.28 us
    ppermute x4, starting transfers between devices, swap(): return lax.ppermute(array, 'vir', [(k, k ^ mask) for k in range(vir)])  4.18 us
  transfers between devices with their start and end apart: 11, of which 5 were waited for; matrix products, arithmetic and copies ran while one was open for 3% of the time, Pallas kernels for 24%

profile of v1, /device:TPU:0, one launch (start us, length us, event | category | flops | bytes accessed | tf_op | source)
XLA Modules:
  0.0 182.5 jit_solution(17101859548005510353)
XLA Ops:
  0.0 1.0 slice.3
  1.0 6.0 %collective-permute-start.2 = (bf16[2,64,1536]{2,1,0:T(8,128)(2,1)S(1)}, bf16[2,64,1536]{2,1,0:T(8,128)(2,1)S(1)}, u32[]{:S(2)}, u32[]{:S(2)}) collective-permute-start(bf16[2,64,1536]{2,1,0:T(8,128)(2,1)S(1)} %slice.3), channel_id=1, source_target_pairs={{0,2},{4,6},{8,10},{12,14},{16,18},{20,22},{24,26},{28,30}} | collective-permute-start | bytes 1179656 | tf_op jit(solution)/shard_map/ppermute | solution.py:214
  7.0 2.8 %copy.16 = bf16[32,64,512]{2,0,1:T(8,128)(2,1)S(1)} copy(bf16[32,64,512]{2,1,0:T(8,128)(2,1)} %param.4) | data formatting | bytes 4194304 | tf_op args[1]
  9.8 0.1 collective-permute-start
  9.8 6.6 %collective-permute-done.2 = bf16[2,64,1536]{2,1,0:T(8,128)(2,1)S(1)} collective-permute-done((bf16[2,64,1536]{2,1,0:T(8,128)(2,1)S(1)}, bf16[2,64,1536]{2,1,0:T(8,128)(2,1)S(1)}, u32[]{:S(2)}, u32[]{:S(2)}) %collective-permute-start.2) | collective-permute-done | bytes 393248 | tf_op jit(solution)/shard_map/ppermute | solution.py:214
  16.5 1.0 broadcast_select_fusion
  17.5 1.3 collective-permute-start.3
  18.8 49.8 %collective-permute-done.3 = bf16[2,64,1536]{2,1,0:T(8,128)(2,1)S(1)} collective-permute-done((bf16[2,64,1536]{2,1,0:T(8,128)(2,1)S(1)}, bf16[2,64,1536]{2,1,0:T(8,128)(2,1)S(1)}, u32[]{:S(2)}, u32[]{:S(2)}) %collective-permute-start.3) | collective-permute-done | bytes 393248 | tf_op jit(solution)/shard_map/ppermute | solution.py:214
  68.7 1.6 collective-permute-start.4
  70.3 1.5 collective-permute-start.5
  71.8 1.3 collective-permute-start.1
  73.1 7.1 %collective-permute-start.10 = (bf16[64,32,512]{2,1,0:T(8,128)(2,1)S(1)}, bf16[64,32,512]{2,1,0:T(8,128)(2,1)}, u32[]{:S(2)}, u32[]{:S(2)}) collective-permute-start(bf16[64,32,512]{2,1,0:T(8,128)(2,1)S(1)} %bitcast.16), channel_id=1, source_target_pairs={{3,2},{0,1},{7,6},{4,5},{11,10},{8,9},{15,14},{12,13},{19,18},{16,... | collective-permute-start | bytes 6291464 | tf_op jit(solution)/shard_map/ppermute | solution.py:246
  80.2 0.0 collective-permute-done.4.refs_1_
  80.2 2.0 %collective-permute-start.9 = (bf16[64,32,512]{2,1,0:T(8,128)(2,1)S(1)}, bf16[64,32,512]{2,1,0:T(8,128)(2,1)}, u32[]{:S(2)}, u32[]{:S(2)}) collective-permute-start(bf16[64,32,512]{2,1,0:T(8,128)(2,1)S(1)} %bitcast.17), channel_id=1, source_target_pairs={{2,1},{1,2},{6,5},{5,6},{10,9},{9,10},{14,13},{13,14},{18,17},{17,... | collective-permute-start | bytes 6291464 | tf_op jit(solution)/shard_map/ppermute | solution.py:246
  82.2 0.0 collective-permute-done
  82.2 1.3 collective-permute-start.8
  83.5 0.0 collective-permute-done.5.refs_2_
  83.5 1.1 collective-permute-start.6
  84.6 9.0 %collective-permute-done.6.refs_3_ = bf16[2,64,1536]{2,1,0:T(8,128)(2,1)S(1)} collective-permute-done((bf16[2,64,1536]{2,1,0:T(8,128)(2,1)S(1)}, bf16[2,64,1536]{2,1,0:T(8,128)(2,1)S(1)}, u32[]{:S(2)}, u32[]{:S(2)}) %collective-permute-start.6) | collective-permute-done | bytes 393248 | tf_op jit(solution)/shard_map/ppermute | solution.py:225
  93.6 1.3 shard_map.37
  94.9 0.0 collective-permute-start.7
  94.9 0.1 stack.35.refs_0_
  95.0 0.7 dynamic-slice_bitcast_fusion.refs_0_
  95.6 3.0 %collective-permute-done.7.refs_2_ = bf16[4,2,64,1536]{3,2,1,0:T(8,128)(2,1)} collective-permute-done((bf16[4,2,64,1536]{3,2,1,0:T(8,128)(2,1)}, bf16[4,2,64,1536]{3,2,1,0:T(8,128)(2,1)}, u32[]{:S(2)}, u32[]{:S(2)}) %collective-permute-start.7) | collective-permute-done | bytes 1572896 | tf_op jit(solution)/shard_map/ppermute | solution.py:225
  98.6 3.0 %shard_map.38 = (bf16[2,1536,512]{2,1,0:T(8,128)(2,1)S(1)}, f32[8,128]{1,0:T(8,128)S(1)}) custom-call(s32[8]{0:T(128)S(1)} %stack.35.refs_0_, bf16[4,2,64,1536]{3,2,1,0:T(8,128)(2,1)} %get-tuple-element.14.refs_1_, bf16[4,2,64,1536]{3,2,1,0:T(8,128)(2,1)} %collective-permute-done.7.refs_2_, ...), custom_call_target="tpu_custom_call", output_to_operand_aliasing={{1}: (3, {})} | custom-call | flops 1024 | bytes 1024 | tf_op jit(solution)/shard_map/pallas_call | solution.py:32
  101.6 31.1 %shard_map.39 = (bf16[64,2,128,512]{3,2,1,0:T(8,128)(2,1)S(1)}, f32[8,128]{1,0:T(8,128)S(1)}) custom-call(bf16[128,64,1536]{2,1,0:T(8,128)(2,1)} %refs_0_.1, bf16[2,1536,512]{2,1,0:T(8,128)(2,1)S(1)} %get-tuple-element.16.refs_1_, f32[8,128]{1,0:T(8,128)S(1)} %get-tuple-element.17.refs_2_), custom_call_target="tpu_custom_call", output_to_operand_aliasing={{1}: (2, {})} | custom-call | flops 1024 | bytes 1024 | tf_op jit(solution)/shard_map/pallas_call | solution.py:32
  132.7 0.0 collective-permute-done.1.refs_2_
  132.7 7.9 %shard_map.40 = (f32[96,256]{1,0:T(8,128)S(1)}, f32[8,128]{1,0:T(8,128)S(1)}) custom-call(bf16[64,32,512]{2,1,0:T(8,128)(2,1)S(1)} %bitcast.18, bf16[64,32,512]{2,1,0:T(8,128)(2,1)} %bitcast.2.refs_1_, bf16[64,32,512]{2,1,0:T(8,128)(2,1)} %collective-permute-done.1.refs_2_, ...), custom_call_target="tpu_custom_call", output_to_operand_aliasing={{1}: (4, {})} | custom-call | flops 1024 | bytes 1024 | tf_op jit(solution)/shard_map/pallas_call | solution.py:32
  140.6 0.0 collective-permute-done.10.refs_4_
  140.6 0.0 collective-permute-done.9.refs_3_
  140.6 24.9 %collective-permute-done.8.refs_2_ = bf16[64,32,512]{2,1,0:T(8,128)(2,1)} collective-permute-done((bf16[64,32,512]{2,1,0:T(8,128)(2,1)}, bf16[64,32,512]{2,1,0:T(8,128)(2,1)}, u32[]{:S(2)}, u32[]{:S(2)}) %collective-permute-start.8) | collective-permute-done | bytes 2097184 | tf_op jit(solution)/shard_map/ppermute | solution.py:246
  165.6 8.3 %shard_map.41 = (f32[128,256]{1,0:T(8,128)S(1)}, f32[8,128]{1,0:T(8,128)S(1)}) custom-call(s32[4]{0:T(128)S(1)} %dynamic-slice_bitcast_fusion.refs_0_, f32[96,256]{1,0:T(8,128)S(1)} %get-tuple-element.20.refs_1_, bf16[64,32,512]{2,1,0:T(8,128)(2,1)} %collective-permute-done.8.refs_2_, ...), custom_call_target="tpu_custom_call", output_to_operand_aliasing={{1}: (6, {})} | custom-call | flops 1024 | bytes 1024 | tf_op jit(solution)/shard_map/pallas_call | solution.py:32
  173.9 7.9 %all_to_all.5 = f32[8,16,256]{2,1,0:T(8,128)S(1)} all-to-all(f32[8,16,256]{2,1,0:T(8,128)S(1)} %bitcast.19), channel_id=1, replica_groups=mesh['vir'=8,'out'=4] {'vir'}, dimensions={0} | all-to-all | bytes 262144 | tf_op jit(solution)/shard_map/all_to_all | solution.py:270
  181.9 0.6 copy.13
  (4 shorter events, 0.1 us)
Async XLA Ops:
  1.0 15.4 %collective-permute-start.2 = (bf16[2,64,1536]{2,1,0:T(8,128)(2,1)S(1)}, bf16[2,64,1536]{2,1,0:T(8,128)(2,1)S(1)}, u32[]{:S(2)}, u32[]{:S(2)}) collective-permute-start(bf16[2,64,1536]{2,1,0:T(8,128)(2,1)S(1)} %slice.3), channel_id=1, source_target_pairs={{0,2},{4,6},{8,10},{12,14},{16,18},{20,22},{24,26},{28,30}} | collective-permute-start | bytes 1179656 | tf_op jit(solution)/shard_map/ppermute | solution.py:214
  9.8 72.4 %collective-permute-start = (bf16[32,64,512]{2,0,1:T(8,128)(2,1)S(1)}, bf16[32,64,512]{2,0,1:T(8,128)(2,1)}, u32[]{:S(2)}, u32[]{:S(2)}) collective-permute-start(bf16[32,64,512]{2,0,1:T(8,128)(2,1)S(1)} %copy.16), channel_id=1, source_target_pairs={{3,1},{1,0},{0,2},{2,3},{7,5},{5,4},{4,6},{6,7},{11,9},{9,8},{8,10... | collective-permute-start | bytes 6291464 | tf_op jit(solution)/shard_map/ppermute | solution.py:246
  17.5 51.2 %collective-permute-start.3 = (bf16[2,64,1536]{2,1,0:T(8,128)(2,1)S(1)}, bf16[2,64,1536]{2,1,0:T(8,128)(2,1)S(1)}, u32[]{:S(2)}, u32[]{:S(2)}) collective-permute-start(bf16[2,64,1536]{2,1,0:T(8,128)(2,1)S(1)} %broadcast_select_fusion), channel_id=1, source_target_pairs={{0,1},{2,3},{4,5},{6,7},{8,9},{10,11},{12,13},{14,15},{16,17},{18,... | collective-permute-start | bytes 1179656 | tf_op jit(solution)/shard_map/ppermute | solution.py:214
  68.7 11.5 %collective-permute-start.4 = (bf16[2,64,1536]{2,1,0:T(8,128)(2,1)S(1)}, bf16[2,64,1536]{2,1,0:T(8,128)(2,1)S(1)}, u32[]{:S(2)}, u32[]{:S(2)}) collective-permute-start(bf16[2,64,1536]{2,1,0:T(8,128)(2,1)S(1)} %broadcast_select_fusion.1.refs_0_), channel_id=1, source_target_pairs={{0,8},{4,12},{8,0},{12,4},{16,24},{20,28},{24,16},{28,20},{1,9},{5... | collective-permute-start | bytes 1179656 | tf_op jit(solution)/shard_map/ppermute | solution.py:225
  70.3 13.2 %collective-permute-start.5 = (bf16[2,64,1536]{2,1,0:T(8,128)(2,1)S(1)}, bf16[2,64,1536]{2,1,0:T(8,128)(2,1)S(1)}, u32[]{:S(2)}, u32[]{:S(2)}) collective-permute-start(bf16[2,64,1536]{2,1,0:T(8,128)(2,1)S(1)} %broadcast_select_fusion.1.refs_0_), channel_id=1, source_target_pairs={{0,16},{4,20},{8,24},{12,28},{16,0},{20,4},{24,8},{28,12},{1,17},{... | collective-permute-start | bytes 1179656 | tf_op jit(solution)/shard_map/ppermute | solution.py:225
  71.8 60.9 %collective-permute-start.1 = (bf16[64,32,512]{2,1,0:T(8,128)(2,1)S(1)}, bf16[64,32,512]{2,1,0:T(8,128)(2,1)}, u32[]{:S(2)}, u32[]{:S(2)}) collective-permute-start(bf16[64,32,512]{2,1,0:T(8,128)(2,1)S(1)} %bitcast.15), channel_id=1, source_target_pairs={{2,0},{1,3},{6,4},{5,7},{10,8},{9,11},{14,12},{13,15},{18,16},{17,... | collective-permute-start | bytes 6291464 | tf_op jit(solution)/shard_map/ppermute | solution.py:246
  73.1 67.5 %collective-permute-start.10 = (bf16[64,32,512]{2,1,0:T(8,128)(2,1)S(1)}, bf16[64,32,512]{2,1,0:T(8,128)(2,1)}, u32[]{:S(2)}, u32[]{:S(2)}) collective-permute-start(bf16[64,32,512]{2,1,0:T(8,128)(2,1)S(1)} %bitcast.16), channel_id=1, source_target_pairs={{3,2},{0,1},{7,6},{4,5},{11,10},{8,9},{15,14},{12,13},{19,18},{16,... | collective-permute-start | bytes 6291464 | tf_op jit(solution)/shard_map/ppermute | solution.py:246
  80.2 60.4 %collective-permute-start.9 = (bf16[64,32,512]{2,1,0:T(8,128)(2,1)S(1)}, bf16[64,32,512]{2,1,0:T(8,128)(2,1)}, u32[]{:S(2)}, u32[]{:S(2)}) collective-permute-start(bf16[64,32,512]{2,1,0:T(8,128)(2,1)S(1)} %bitcast.17), channel_id=1, source_target_pairs={{2,1},{1,2},{6,5},{5,6},{10,9},{9,10},{14,13},{13,14},{18,17},{17,... | collective-permute-start | bytes 6291464 | tf_op jit(solution)/shard_map/ppermute | solution.py:246
  82.2 83.4 %collective-permute-start.8 = (bf16[64,32,512]{2,1,0:T(8,128)(2,1)}, bf16[64,32,512]{2,1,0:T(8,128)(2,1)}, u32[]{:S(2)}, u32[]{:S(2)}) collective-permute-start(bf16[64,32,512]{2,1,0:T(8,128)(2,1)} %bitcast.2.refs_1_), channel_id=1, source_target_pairs={{1,0},{2,3},{5,4},{6,7},{9,8},{10,11},{13,12},{14,15},{17,16},{18,... | collective-permute-start | bytes 6291464 | tf_op jit(solution)/shard_map/ppermute | solution.py:246
  83.5 10.1 %collective-permute-start.6 = (bf16[2,64,1536]{2,1,0:T(8,128)(2,1)S(1)}, bf16[2,64,1536]{2,1,0:T(8,128)(2,1)S(1)}, u32[]{:S(2)}, u32[]{:S(2)}) collective-permute-start(bf16[2,64,1536]{2,1,0:T(8,128)(2,1)S(1)} %broadcast_select_fusion.1.refs_0_), channel_id=1, source_target_pairs={{0,24},{4,28},{8,16},{12,20},{16,8},{20,12},{24,0},{28,4},{1,25},{... | collective-permute-start | bytes 1179656 | tf_op jit(solution)/shard_map/ppermute | solution.py:225
  94.9 3.8 %collective-permute-start.7 = (bf16[4,2,64,1536]{3,2,1,0:T(8,128)(2,1)}, bf16[4,2,64,1536]{3,2,1,0:T(8,128)(2,1)}, u32[]{:S(2)}, u32[]{:S(2)}) collective-permute-start(bf16[4,2,64,1536]{3,2,1,0:T(8,128)(2,1)} %get-tuple-element.14.refs_1_), channel_id=1, source_target_pairs={{0,4},{4,0},{8,12},{12,8},{16,20},{20,16},{24,28},{28,24},{1,5},{5... | collective-permute-start | bytes 4718600 | tf_op jit(solution)/shard_map/ppermute | solution.py:225
